TPU v7x, 32 devices: a whole 2x2x4 slice. The times are simulated.
32 devices in a mesh: parts: 2 (over x), wide: 16 (over z, y, core).
Axes of the slice: x: 2, y: 2, z: 4, core: 2. Of those that a mesh axis runs over, the one named last changes fastest.
Arguments:
- tokens: bfloat16 [8192, 2048], P(('parts', 'wide')), parts along dimension 0, may hold values from -6 to 6
- token_group: int32 [8192], P(('parts', 'wide')), parts along dimension 0, may hold values from 0 to 255, as said below
- group_experts: int32 [512, 1], P(('parts', 'wide')), parts along dimension 0, may hold values from -1 to 15, as said below
- route_ids: int32 [8192, 8], P(('parts', 'wide')), parts along dimension 0, may hold values from 0 to 15, as said below
- route_gates: float32 [8192, 8], P(('parts', 'wide')), parts along dimension 0, may hold values from 0.1 to 1
- w_gate: bfloat16 [16, 2048, 768], P('wide'), may hold values from -0.125 to 0.125
- w_up: bfloat16 [16, 2048, 768], P('wide'), may hold values from -0.125 to 0.125
- w_down: bfloat16 [16, 768, 2048], P('wide'), may hold values from -0.21875 to 0.21875
Outputs:
- mixed: bfloat16 [8192, 2048], P(('parts', 'wide')), parts along dimension 0
There are 2 independent parts, one for each index of `parts`. A program takes and returns all parts, laid end to end along the dimension named above; an argument that names none is the same for every part. Nothing has to cross between parts.
Inputs may be any that keep to these rules, and one draw needn't show every extreme that they name: `token_group`: Nondecreasing. The 256 tokens of index d of wide form groups d * 16 to d * 16 + 15, each a run of 1 to 24 tokens; on every index one group has exactly 24 tokens. `group_experts`: row g holds 2 to 1 distinct experts in its first entries and -1 after them; the groups of one index of wide list disjoint experts; every index has a group of 1 expert holding 24 tokens. Hence at most 24 tokens of one index of wide are kept for one expert, and one expert gets exactly 24 from every index. `route_ids`: each row names 8 distinct experts, among them every expert listed for the token's group.
All inputs are finite; a program needn't handle non-finite values.
Results may differ from a plain program's by a relative error of at most 0.0058.
Values may be sent and summed in bfloat16 or wider, within the bound.
A program may use at most 128 MiB of HBM per device.

v0:
```python
import functools

import jax
import jax.numpy as jnp
from jax import lax
from jax.experimental import pallas as pl
from jax.experimental.pallas import tpu as pltpu
from jax.sharding import PartitionSpec as P

CAP = 24
MESH = pl.DeviceIdType.MESH
SEND_ORDER = (3, 2, 1, 0)
WORK_ORDER = (3, 2, 1, 0)
TAKE_ORDER = (3, 2, 1, 0)


def partner(me, distance):
    other = me
    bit = 1
    while bit <= distance:
        if distance & bit:
            other = other + bit * (1 - 2 * (lax.div(me, bit) % 2))
        bit *= 2
    return other


def kernel(
    n, chunks, tokens_ref, group_ref, listed_ref, ids_ref, gates_ref, gate_hbm, up_hbm, down_hbm, out_ref,
    gate_w, up_w, down_w, outgoing, arrived, results, back, hidden, total, weight_sem, send_a, recv_a, send_b, recv_b,
):
    me = lax.axis_index("wide")
    count, width = tokens_ref.shape
    groups, lists = listed_ref.shape
    per = n // chunks
    rows = per * CAP
    inner = hidden.shape[1]

    barrier = pltpu.get_barrier_semaphore()
    for d in range(1, n):
        pl.semaphore_signal(barrier, inc=1, device_id={"wide": partner(me, d)}, device_id_type=MESH)
    loads = [
        pltpu.make_async_copy(src.at[0], dst, weight_sem.at[i])
        for i, (src, dst) in enumerate(((gate_hbm, gate_w), (up_hbm, up_w), (down_hbm, down_w)))
    ]

    local = group_ref[...] - me * groups
    group_iota = lax.broadcasted_iota(jnp.int32, (groups, count), 0)
    in_group = local == group_iota
    starts = jnp.sum((local < group_iota).astype(jnp.float32), axis=1, keepdims=True)
    start_row = jnp.sum(jnp.where(in_group, starts, 0.0), axis=0, keepdims=True).astype(jnp.int32)
    slot_row = lax.broadcasted_iota(jnp.int32, (1, count), 1) - start_row
    experts, targets = [], []
    for index in range(lists):
        named = listed_ref[:, index : index + 1].astype(jnp.float32) + 1.0
        expert = jnp.sum(jnp.where(in_group, named, 0.0), axis=0, keepdims=True).astype(jnp.int32) - 1
        block = jnp.bitwise_xor(expert, jnp.full((1, count), me, jnp.int32))
        experts.append(expert)
        targets.append(jnp.where(expert >= 0, block * CAP + slot_row, -1))

    def copy(phase, d):
        src, dst, send, recv = ((outgoing, arrived, send_a, recv_a), (results, back, send_b, recv_b))[phase]
        return pltpu.make_async_remote_copy(
            src_ref=src.at[d],
            dst_ref=dst.at[d],
            send_sem=send.at[d],
            recv_sem=recv.at[d],
            device_id={"wide": partner(me, d)},
            device_id_type=MESH,
        )

    def members(c):
        return [d for d in range(c * per, (c + 1) * per) if d > 0]

    greeted = False
    for c in SEND_ORDER:
        row_iota = lax.broadcasted_iota(jnp.int32, (rows, count), 0) + c * rows
        pick = sum((row_iota == target).astype(jnp.float32) for target in targets).astype(jnp.bfloat16)
        tile = min(width, 512)

        def pack(j, carry):
            cols = pl.ds(pl.multiple_of(j * tile, tile), tile)
            picked = jnp.dot(pick, tokens_ref[:, cols], preferred_element_type=jnp.float32)
            outgoing[pl.ds(c * per, per), :, cols] = picked.reshape(per, CAP, tile).astype(jnp.bfloat16)
            return carry

        lax.fori_loop(0, width // tile, pack, 0)
        if not greeted:
            pl.semaphore_wait(barrier, n - 1)
            greeted = True
        for d in reversed(members(c)):
            copy(0, d).start()
    for load in loads:
        load.start()
    own = pltpu.make_async_copy(outgoing.at[0], arrived.at[0], weight_sem.at[3])
    own.start()

    columns = []
    for index in range(lists):
        target = jnp.transpose(jnp.broadcast_to(targets[index].astype(jnp.float32), (128, count)))[:, :1]
        expert = jnp.transpose(jnp.broadcast_to(experts[index].astype(jnp.float32), (128, count)))[:, :1]
        expert = expert.astype(jnp.int32)
        chosen = jnp.where(ids_ref[...] == expert, gates_ref[...], 0.0)
        weight = jnp.where(expert >= 0, jnp.sum(chosen, axis=1, keepdims=True), 0.0)
        columns.append((target.astype(jnp.int32), weight))

    loaded = False
    for c in WORK_ORDER:
        for d in members(c):
            copy(0, d).wait_recv()
        if c == 0:
            own.wait()
        if not loaded:
            for load in loads:
                load.wait()
            loaded = True

        def raise_(j, carry):
            cols = pl.ds(pl.multiple_of(j * 256, 256), 256)
            x = arrived[pl.ds(c * per, per)].reshape(rows, width)
            gate = jnp.dot(x, gate_w[:, cols], preferred_element_type=jnp.float32)
            upper = jnp.dot(x, up_w[:, cols], preferred_element_type=jnp.float32)
            hidden[:, cols] = (gate / (1.0 + jnp.exp(-gate)) * upper).astype(jnp.bfloat16)
            return carry

        lax.fori_loop(0, inner // 256, raise_, 0)

        def lower(j, carry):
            cols = pl.ds(pl.multiple_of(j * 512, 512), 512)
            y = jnp.dot(hidden[...], down_w[:, cols], preferred_element_type=jnp.float32)
            results[pl.ds(c * per, per), :, cols] = y.reshape(per, CAP, 512).astype(jnp.bfloat16)
            return carry

        lax.fori_loop(0, width // 512, lower, 0)
        for d in reversed(members(c)):
            copy(1, d).start()

    for place, c in enumerate(TAKE_ORDER):
        for d in members(c):
            copy(1, d).wait_recv()
        lane_iota = lax.broadcasted_iota(jnp.int32, (count, rows), 1) + c * rows
        picks = [((lane_iota == target).astype(jnp.bfloat16), weight) for target, weight in columns]

        def take(j, carry):
            cols = pl.ds(pl.multiple_of(j * 512, 512), 512)
            own_results = results if c == 0 else None
            y = back[pl.ds(c * per, per), :, cols]
            if own_results is not None:
                y = jnp.concatenate([results[pl.ds(0, 1), :, cols], back[pl.ds(1, per - 1), :, cols]], axis=0)
            y = y.reshape(rows, 512)
            mix = sum(weight * jnp.dot(pick, y, preferred_element_type=jnp.float32) for pick, weight in picks)
            if place > 0:
                mix = mix + total[:, cols]
            if place < chunks - 1:
                total[:, cols] = mix
            else:
                out_ref[:, cols] = mix.astype(jnp.bfloat16)
            return carry

        lax.fori_loop(0, width // 512, take, 0)
    for d in range(1, n):
        copy(0, d).wait_send()
        copy(1, d).wait_send()


def on_device(tokens, token_group, group_experts, route_ids, route_gates, w_gate, w_up, w_down):
    n = lax.axis_size("wide")
    count, width = tokens.shape
    inner = w_gate.shape[2]
    chunks = 4
    vmem = pl.BlockSpec(memory_space=pltpu.VMEM)
    hbm = pl.BlockSpec(memory_space=pl.ANY)
    blocks = pltpu.VMEM((n, CAP, width), jnp.bfloat16)
    return pl.pallas_call(
        functools.partial(kernel, n, chunks),
        out_shape=jax.ShapeDtypeStruct((count, width), jnp.bfloat16),
        in_specs=[vmem] * 5 + [hbm] * 3,
        out_specs=vmem,
        scratch_shapes=[
            pltpu.VMEM((width, inner), jnp.bfloat16),
            pltpu.VMEM((width, inner), jnp.bfloat16),
            pltpu.VMEM((inner, width), jnp.bfloat16),
            blocks,
            blocks,
            blocks,
            blocks,
            pltpu.VMEM((n // chunks * CAP, inner), jnp.bfloat16),
            pltpu.VMEM((count, width), jnp.float32),
            pltpu.SemaphoreType.DMA((4,)),
            pltpu.SemaphoreType.DMA((n,)),
            pltpu.SemaphoreType.DMA((n,)),
            pltpu.SemaphoreType.DMA((n,)),
            pltpu.SemaphoreType.DMA((n,)),
        ],
        compiler_params=pltpu.CompilerParams(
            collective_id=0, has_side_effects=True, vmem_limit_bytes=56 * 1024 * 1024
        ),
        cost_estimate=pl.CostEstimate(
            flops=6 * n * CAP * width * inner, bytes_accessed=6 * width * inner + 4 * count * width,
            transcendentals=n * CAP * inner,
        ),
    )(tokens, token_group.reshape(1, count), group_experts, route_ids, route_gates, w_gate, w_up, w_down)


def solution(mesh):
    in_specs = (
        P(("parts", "wide"), None),
        P(("parts", "wide")),
        P(("parts", "wide"), None),
        P(("parts", "wide"), None),
        P(("parts", "wide"), None),
        P("wide", None, None),
        P("wide", None, None),
        P("wide", None, None),
    )
    out_specs = P(("parts", "wide"), None)
    return jax.shard_map(
        on_device, mesh=mesh, in_specs=in_specs, out_specs=out_specs, check_vma=False
    )
```

profile of v0, /device:TPU:0, one launch (start us, length us, event | category | flops | bytes accessed | tf_op | source)
XLA Modules:
  0.0 89.4 jit_solution(9579754079500052959)
XLA Ops:
  0.0 1.3 %copy.9.listed_ref = s32[16,1]{1,0:T(8,128)} copy(s32[16,1]{0,1:T(1,128)} %param.10) | data formatting | bytes 128 | tf_op args[2]
  1.3 1.5 %copy.10.ids_ref = s32[256,8]{1,0:T(8,128)} copy(s32[256,8]{0,1:T(8,128)} %param.11) | data formatting | bytes 16384 | tf_op args[3]
  2.8 1.5 %copy.11.gates_ref = f32[256,8]{1,0:T(8,128)} copy(f32[256,8]{0,1:T(8,128)} %param.12) | data formatting | bytes 16384 | tf_op args[4]
  4.3 82.8 %shard_map.82 = bf16[256,2048]{1,0:T(8,128)(2,1)} custom-call(bf16[256,2048]{1,0:T(8,128)(2,1)} %tokens_ref.1, s32[1,256]{1,0:T(1,128)} %bitcast.1, s32[16,1]{1,0:T(8,128)} %copy.9.listed_ref, s32[256,8]{1,0:T(8,128)} %copy.10.ids_ref, f32[256,8]{1,0:T(8,128)} %copy.11.gates_ref, bf16[1,2048,768]{2,1,0:T(8,128)(2,1)} %gate_hbm.1, ...), custom_call_target="tpu_custom_call" | custom-call | flops 3623878656 | bytes 11534336 | tf_op jit(solution)/shard_map/pallas_call | solution.py:173
  87.1 2.3 %copy.13 = bf16[256,2048]{1,0:T(8,128)(2,1)} copy(bf16[256,2048]{1,0:T(8,128)(2,1)} %shard_map.82) | data formatting | bytes 2097152
where the time goes:
time: 89.6 us; the launch traced here: 89.4 us
  Pallas kernels  82.8 us (92%)
  local copies, waits for them, and re-layouts  6.58 us (7%)
    pallas_call x1, Pallas kernels, on_device(): pl.pallas_call(functools.partial(kernel, n, chunks), out_shape=jax.ShapeD...  82.8 us
    unnamed x4, local copies, waits for them, and re-layouts  6.58 us

commit v1 on v0

--- a/solution.py
+++ b/solution.py
@@ -9,9 +9,9 @@
 
 CAP = 24
 MESH = pl.DeviceIdType.MESH
-SEND_ORDER = (3, 2, 1, 0)
-WORK_ORDER = (3, 2, 1, 0)
-TAKE_ORDER = (3, 2, 1, 0)
+SEND_ORDER = (2, 3, 1, 0)
+WORK_ORDER = (2, 1, 3, 0)
+TAKE_ORDER = (1, 2, 0, 3)
 
 
 def partner(me, distance):
@@ -30,7 +30,7 @@
 ):
     me = lax.axis_index("wide")
     count, width = tokens_ref.shape
-    groups, lists = listed_ref.shape
+    lists, groups = listed_ref.shape
     per = n // chunks
     rows = per * CAP
     inner = hidden.shape[1]
@@ -49,9 +49,14 @@
     starts = jnp.sum((local < group_iota).astype(jnp.float32), axis=1, keepdims=True)
     start_row = jnp.sum(jnp.where(in_group, starts, 0.0), axis=0, keepdims=True).astype(jnp.int32)
     slot_row = lax.broadcasted_iota(jnp.int32, (1, count), 1) - start_row
+    diagonal = lax.broadcasted_iota(jnp.int32, (groups, groups), 0) == lax.broadcasted_iota(
+        jnp.int32, (groups, groups), 1
+    )
     experts, targets = [], []
     for index in range(lists):
-        named = listed_ref[:, index : index + 1].astype(jnp.float32) + 1.0
+        named = jnp.sum(
+            jnp.where(diagonal, listed_ref[index : index + 1, :].astype(jnp.float32) + 1.0, 0.0), axis=1, keepdims=True
+        )
         expert = jnp.sum(jnp.where(in_group, named, 0.0), axis=0, keepdims=True).astype(jnp.int32) - 1
         block = jnp.bitwise_xor(expert, jnp.full((1, count), me, jnp.int32))
         experts.append(expert)
@@ -96,11 +101,10 @@
 
     columns = []
     for index in range(lists):
+        chosen = jnp.where(ids_ref[...] == experts[index], gates_ref[...], 0.0)
+        weight = jnp.where(experts[index] >= 0, jnp.sum(chosen, axis=0, keepdims=True), 0.0)
+        weight = jnp.transpose(jnp.broadcast_to(weight, (128, count)))[:, :1]
         target = jnp.transpose(jnp.broadcast_to(targets[index].astype(jnp.float32), (128, count)))[:, :1]
-        expert = jnp.transpose(jnp.broadcast_to(experts[index].astype(jnp.float32), (128, count)))[:, :1]
-        expert = expert.astype(jnp.int32)
-        chosen = jnp.where(ids_ref[...] == expert, gates_ref[...], 0.0)
-        weight = jnp.where(expert >= 0, jnp.sum(chosen, axis=1, keepdims=True), 0.0)
         columns.append((target.astype(jnp.int32), weight))
 
     loaded = False
@@ -172,7 +176,7 @@
     blocks = pltpu.VMEM((n, CAP, width), jnp.bfloat16)
     return pl.pallas_call(
         functools.partial(kernel, n, chunks),
-        out_shape=jax.ShapeDtypeStruct((count, width), jnp.bfloat16),
+        out_shape=pltpu.VMEM((count, width), jnp.bfloat16),
         in_specs=[vmem] * 5 + [hbm] * 3,
         out_specs=vmem,
         scratch_shapes=[
@@ -198,7 +202,7 @@
             flops=6 * n * CAP * width * inner, bytes_accessed=6 * width * inner + 4 * count * width,
             transcendentals=n * CAP * inner,
         ),
-    )(tokens, token_group.reshape(1, count), group_experts, route_ids, route_gates, w_gate, w_up, w_down)
+    )(tokens, token_group.reshape(1, count), group_experts.T, route_ids.T, route_gates.T, w_gate, w_up, w_down)
 
 
 def solution(mesh):

time: 89.6 us -> 76.7 us (0.86)
  the two profiles are of different devices: /device:TPU:0 before, /device:TPU:11 now
where the time goes in v1:
time: 76.7 us; the launch traced here: 76.6 us
  Pallas kernels  75.6 us (99%)
  local copies, waits for them, and re-layouts  0.97 us (1%)
    pallas_call x1, Pallas kernels, on_device(): pl.pallas_call(functools.partial(kernel, n, chunks), out_shape=pltpu.VMEM...  75.6 us

profile of v1, /device:TPU:11, one launch (start us, length us, event | category | flops | bytes accessed | tf_op | source)
XLA Modules:
  0.0 76.6 jit_solution(10331701802937264803)
XLA Ops:
  0.0 75.6 %shard_map.82 = bf16[256,2048]{1,0:T(8,128)(2,1)S(1)} custom-call(bf16[256,2048]{1,0:T(8,128)(2,1)} %tokens_ref.1, s32[1,256]{1,0:T(1,128)} %bitcast.6, s32[1,16]{1,0:T(1,128)} %bitcast.7, s32[8,256]{1,0:T(8,128)} %bitcast.4, f32[8,256]{1,0:T(8,128)} %bitcast.5, bf16[1,2048,768]{2,1,0:T(8,128)(2,1)} %gate_hbm.1, bf16[1,2048,768]{2,1,0:T(8,128)(2,1)} %up_hbm.1, ...), custom_call_target="tpu_custom_call" | custom-call | flops 3623878656 | bytes 11534336 | tf_op jit(solution)/shard_map/pallas_call | solution.py:177
  75.6 1.0 %copy.10 = bf16[256,2048]{1,0:T(8,128)(2,1)} copy(bf16[256,2048]{1,0:T(8,128)(2,1)S(1)} %shard_map.82) | data formatting | bytes 2097152

commit v2 on v1

--- a/solution.py
+++ b/solution.py
@@ -10,8 +10,8 @@
 CAP = 24
 MESH = pl.DeviceIdType.MESH
 SEND_ORDER = (2, 3, 1, 0)
-WORK_ORDER = (2, 1, 3, 0)
-TAKE_ORDER = (1, 2, 0, 3)
+WORK_ORDER = (2, 1, 0, 3)
+TAKE_ORDER = (1, 0, 2, 3)
 
 
 def partner(me, distance):

time: 76.7 us -> 76.7 us (level)
  no operation moved by 1% of the time
where the time goes in v2:
time: 76.7 us; the launch traced here: 76.6 us
  Pallas kernels  75.6 us (99%)
  local copies, waits for them, and re-layouts  0.97 us (1%)
    pallas_call x1, Pallas kernels, on_device(): pl.pallas_call(functools.partial(kernel, n, chunks), out_shape=pltpu.VMEM...  75.6 us

profile of v2, /device:TPU:11, one launch (start us, length us, event | category | flops | bytes accessed | tf_op | source)
XLA Modules:
  0.0 76.6 jit_solution(3801653234203538537)
XLA Ops:
  0.0 75.6 %shard_map.82 = bf16[256,2048]{1,0:T(8,128)(2,1)S(1)} custom-call(bf16[256,2048]{1,0:T(8,128)(2,1)} %tokens_ref.1, s32[1,256]{1,0:T(1,128)} %bitcast.6, s32[1,16]{1,0:T(1,128)} %bitcast.7, s32[8,256]{1,0:T(8,128)} %bitcast.4, f32[8,256]{1,0:T(8,128)} %bitcast.5, bf16[1,2048,768]{2,1,0:T(8,128)(2,1)} %gate_hbm.1, bf16[1,2048,768]{2,1,0:T(8,128)(2,1)} %up_hbm.1, ...), custom_call_target="tpu_custom_call" | custom-call | flops 3623878656 | bytes 11534336 | tf_op jit(solution)/shard_map/pallas_call | solution.py:177
  75.6 1.0 %copy.10 = bf16[256,2048]{1,0:T(8,128)(2,1)} copy(bf16[256,2048]{1,0:T(8,128)(2,1)S(1)} %shard_map.82) | data formatting | bytes 2097152
